TPU v7x, 32 devices: a whole 2x2x4 slice. The times are simulated.
32 devices in a mesh: group: 4 (over y, core), leaf: 8 (over z, x).
Axes of the slice: x: 2, y: 2, z: 4, core: 2. Of those that a mesh axis runs over, the one named last changes fastest.
Arguments:
- left_vectors: float32 [256, 128], replicated, may hold values from -6 to 6
- panel_vectors: bfloat16 [2, 256, 128], replicated, may hold values from -0.375 to 0.375
- panel_factors: float32 [2, 128, 128], replicated, may hold values from -0.5 to 0.5
- node_y: bfloat16 [4, 8, 5, 256, 256], P('group', 'leaf')
- node_t: float32 [4, 8, 5, 128, 256], P('group', 'leaf'), as said below
- leaf_v: bfloat16 [16384, 256], P(('group', 'leaf')), may hold values from -0.375 to 0.375
- leaf_t: float32 [4, 8, 256, 256], P('group', 'leaf'), may hold values from -0.1875 to 0.1875
- leaf_map: int32 [4, 8], P('group', 'leaf'), may hold values from 0 to 7, as said below
Outputs:
- eofs: bfloat16 [16384, 128], P(('group', 'leaf'))
Inputs may be any that keep to these rules, and one draw needn't show every extreme that they name: leaf_map[g, s] is the leaf index of the device of group g that holds leaf slot s; slots 2m and 2m + 1 name devices 2m and 2m + 1 in either order. Every device that a node of level l covers holds the same node_y[., ., l]; every device in the first half of the node's devices holds the same node_t[., ., l], and so does every device in the second half.
All inputs are finite; a program needn't handle non-finite values.
Results may differ from a plain program's by a relative error of at most 0.0045.
Values sent between devices are 32-bit elements; how exact they have to be, the bound alone decides.
A program may use at most 64 MiB of HBM per device.

v0:
```python
import jax
import jax.numpy as jnp
from jax import lax
from jax.sharding import PartitionSpec as P

highest = lax.Precision.HIGHEST


def from_partner(block, axis, bit):
    count = lax.axis_size(axis)
    route = []
    for low in range(count):
        high = low | 1 << bit
        if high != low and high < count:
            route += [(low, high), (high, low)]
    return lax.ppermute(block, axis, route)


def back_panels(vectors, panel_vectors, panel_factors):
    result = vectors
    panel_count = panel_vectors.shape[0]
    for panel_index in range(panel_count - 1, -1, -1):
        reflect = panel_vectors[panel_index].astype(jnp.float32)
        projected = lax.dot_general(reflect, result, (((0,), (0,)), ((), ())), precision=highest)
        scaled = jnp.dot(panel_factors[panel_index], projected, precision=highest)
        result = result - jnp.dot(reflect, scaled, precision=highest)
    return result


def stack_rows(own_rows, partner_rows, bottom):
    first = jnp.concatenate([own_rows, partner_rows], axis=0)
    second = jnp.concatenate([partner_rows, own_rows], axis=0)
    return jnp.where(bottom, second, first)


def split_node(vectors, weighted, reflect, take_lower):
    return lax.cond(
        take_lower,
        lambda: -jnp.dot(reflect.astype(jnp.float32), weighted, precision=highest),
        lambda: vectors - weighted,
    )


def on_device(left_vectors, panel_vectors, panel_factors, node_y, node_t, leaf_v, leaf_t, leaf_map):
    slot_count = lax.axis_size("leaf")
    group_count = lax.axis_size("group")
    group_levels = group_count.bit_length() - 1
    leaf_levels = slot_count.bit_length() - 1
    level_count = group_levels + leaf_levels
    group_place = lax.axis_index("group")
    leaf_place = lax.axis_index("leaf")
    current = back_panels(left_vectors, panel_vectors, panel_factors)
    own_factors = node_t[0, 0]
    own_reflect = node_y[0, 0]
    group_steps = [
        (height_index, group_levels - 1 - height_index) for height_index in range(group_levels)
    ]
    leaf_steps = [
        (group_levels + height_index, leaf_levels - 1 - height_index)
        for height_index in range(leaf_levels)
    ]
    flipped = leaf_map[0, 0] != leaf_place
    takes_lower = (leaf_place % 2 == 1) != flipped
    group_partner = [
        from_partner(own_factors[height_index], "group", bit_number)
        for height_index, bit_number in group_steps
    ]
    leaf_partner = [
        from_partner(own_factors[height_index], "leaf", bit_number)
        for height_index, bit_number in leaf_steps
    ]
    for step_index, (height_index, bit_number) in enumerate(group_steps):
        bottom = group_place >> bit_number & 1 == 1
        full_factor = stack_rows(own_factors[height_index], group_partner[step_index], bottom)
        weighted = jnp.dot(full_factor, current, precision=highest)
        current = split_node(current, weighted, own_reflect[height_index], bottom)
    for step_index, (height_index, bit_number) in enumerate(leaf_steps):
        bottom = leaf_place >> bit_number & 1 == 1
        full_factor = stack_rows(own_factors[height_index], leaf_partner[step_index], bottom)
        weighted = jnp.dot(full_factor, current, precision=highest)
        if height_index == level_count - 1:
            current = split_node(current, weighted, own_reflect[height_index], takes_lower)
        else:
            current = split_node(current, weighted, own_reflect[height_index], bottom)
    snapshots = leaf_t.shape[-1]
    factor_leaf = leaf_t[0, 0]
    rounded = current.astype(jnp.bfloat16)
    projected = lax.dot_general(
        leaf_v[:snapshots], rounded, (((0,), (0,)), ((), ())), preferred_element_type=jnp.float32
    )
    solved = jnp.dot(factor_leaf, projected, precision=highest).astype(jnp.bfloat16)
    applied = jnp.dot(leaf_v, solved, preferred_element_type=jnp.float32)
    extended = jnp.pad(current, ((0, leaf_v.shape[0] - snapshots), (0, 0)))
    return (extended - applied).astype(jnp.bfloat16)


def solution(mesh):
    return jax.shard_map(
        on_device,
        mesh=mesh,
        in_specs=(
            P(),
            P(),
            P(),
            P("group", "leaf", None, None, None),
            P("group", "leaf", None, None, None),
            P(("group", "leaf"), None),
            P("group", "leaf", None, None),
            P("group", "leaf"),
        ),
        out_specs=P(("group", "leaf"), None),
        check_vma=False,
    )
```

profile of v0, /device:TPU:0, one launch (start us, length us, event | category | flops | bytes accessed | tf_op | source)
XLA Modules:
  0.0 18.6 jit_solution(16837485093691992473)
XLA Ops:
  0.0 1.3 %slice_bitcast_fusion = (f32[128,256]{1,0:T(8,128)S(1)}, f32[128,256]{1,0:T(8,128)S(1)}, f32[128,256]{1,0:T(8,128)S(1)}, f32[128,256]{1,0:T(8,128)S(1)}, f32[128,256]{1,0:T(8,128)S(1)}) fusion(f32[1,1,5,128,256]{4,3,2,1,0:T(8,128)} %param.22), kind=kLoop, calls=%fused_computation.61 | loop fusion | bytes 1310720 | tf_op jit(solution)/shard_map/squeeze | solution.py:69
  1.3 3.0 %collective-permute-start = (f32[128,256]{1,0:T(8,128)S(1)}, f32[128,256]{1,0:T(8,128)S(1)}, u32[]{:S(2)}, u32[]{:S(2)}) collective-permute-start(f32[128,256]{1,0:T(8,128)S(1)} %get-tuple-element.95), channel_id=1, source_target_pairs={{0,16},{16,0},{8,24},{24,8},{1,17},{17,1},{9,25},{25,9},{2,18},{18... | collective-permute-start | bytes 393224 | tf_op jit(solution)/shard_map/ppermute | solution.py:16
  4.3 2.6 %collective-permute-start.2 = (f32[128,256]{1,0:T(8,128)S(1)}, f32[128,256]{1,0:T(8,128)S(1)}, u32[]{:S(2)}, u32[]{:S(2)}) collective-permute-start(f32[128,256]{1,0:T(8,128)S(1)} %get-tuple-element.93), channel_id=1, source_target_pairs={{0,4},{4,0},{1,5},{5,1},{2,6},{6,2},{3,7},{7,3},{8,12},{12,8},{9,1... | collective-permute-start | bytes 393224 | tf_op jit(solution)/shard_map/ppermute | solution.py:16
  6.9 1.6 %collective-permute-start.3 = (f32[128,256]{1,0:T(8,128)S(1)}, f32[128,256]{1,0:T(8,128)S(1)}, u32[]{:S(2)}, u32[]{:S(2)}) collective-permute-start(f32[128,256]{1,0:T(8,128)S(1)} %get-tuple-element.96), channel_id=1, source_target_pairs={{0,2},{2,0},{1,3},{3,1},{4,6},{6,4},{5,7},{7,5},{8,10},{10,8},{9,1... | collective-permute-start | bytes 393224 | tf_op jit(solution)/shard_map/ppermute | solution.py:16
  8.5 1.5 %collective-permute-start.4 = (f32[128,256]{1,0:T(8,128)S(1)}, f32[128,256]{1,0:T(8,128)S(1)}, u32[]{:S(2)}, u32[]{:S(2)}) collective-permute-start(f32[128,256]{1,0:T(8,128)S(1)} %get-tuple-element.92), channel_id=1, source_target_pairs={{0,1},{1,0},{2,3},{3,2},{4,5},{5,4},{6,7},{7,6},{8,9},{9,8},{10,11... | collective-permute-start | bytes 393224 | tf_op jit(solution)/shard_map/ppermute | solution.py:16
  10.1 0.8 %copy-done.4 = bf16[2,256,128]{2,1,0:T(8,128)(2,1)S(1)} copy-done((bf16[2,256,128]{2,1,0:T(8,128)(2,1)S(1)}, bf16[2,256,128]{2,1,0:T(8,128)(2,1)}, u32[]{:S(2)}) %copy-start.4) | copy-done | bytes 131096
  10.9 0.3 %fusion.60 = f32[128,128]{1,0:T(8,128)S(1)} fusion(f32[256,128]{1,0:T(8,128)S(1)} %copy-done.3, bf16[2,256,128]{2,1,0:T(8,128)(2,1)S(1)} %copy-done.4), kind=kOutput, calls=%fused_computation.79 | convolution fusion | flops 50331648 | bytes 262144 | tf_op jit(solution)/shard_map/dot_general | solution.py:24
  11.1 0.6 %copy-done.5 = f32[2,128,128]{2,1,0:T(8,128)S(1)} copy-done((f32[2,128,128]{2,1,0:T(8,128)S(1)}, f32[2,128,128]{2,1,0:T(8,128)}, u32[]{:S(2)}) %copy-start.5) | copy-done | bytes 131096
  11.8 0.3 %fusion.57 = f32[128,128]{1,0:T(8,128)S(1)} fusion(f32[128,128]{1,0:T(8,128)S(1)} %fusion.60, f32[2,128,128]{2,1,0:T(8,128)S(1)} %copy-done.5), kind=kOutput, calls=%fused_computation.76 | convolution fusion | flops 25165824 | bytes 196608 | tf_op jit(solution)/shard_map/dot_general | solution.py:25
  12.1 0.2 %fusion.13 = f32[256,128]{0,1:T(8,128)S(1)} fusion(f32[256,128]{0,1:T(8,128)S(1)} %copy.9, f32[128,128]{1,0:T(8,128)S(1)} %fusion.57, bf16[2,256,128]{2,1,0:T(8,128)(2,1)S(1)} %copy-done.4), kind=kOutput, calls=%fused_computation.21 | convolution fusion | flops 50364416 | bytes 393216 | tf_op jit(solution)/shard_map/dot_general | solution.py:26
  12.3 0.2 %fusion.55 = f32[128,128]{1,0:T(8,128)S(1)} fusion(f32[256,128]{0,1:T(8,128)S(1)} %fusion.13, bf16[2,256,128]{2,1,0:T(8,128)(2,1)S(1)} %copy-done.4), kind=kOutput, calls=%fused_computation.74 | convolution fusion | flops 50331648 | bytes 262144 | tf_op jit(solution)/shard_map/dot_general | solution.py:24
  12.5 0.3 %fusion.52 = f32[128,128]{1,0:T(8,128)S(1)} fusion(f32[128,128]{1,0:T(8,128)S(1)} %fusion.55, f32[2,128,128]{2,1,0:T(8,128)S(1)} %copy-done.5), kind=kOutput, calls=%fused_computation.71 | convolution fusion | flops 25165824 | bytes 196608 | tf_op jit(solution)/shard_map/dot_general | solution.py:25
  13.5 0.2 %fusion.12 = f32[256,128]{0,1:T(8,128)S(1)} fusion(f32[256,128]{0,1:T(8,128)S(1)} %fusion.13, f32[128,128]{1,0:T(8,128)S(1)} %fusion.52, bf16[2,256,128]{2,1,0:T(8,128)(2,1)S(1)} %copy-done.4), kind=kOutput, calls=%fused_computation.19 | convolution fusion | flops 50364416 | bytes 393216 | tf_op jit(solution)/shard_map/dot_general | solution.py:26
  13.7 0.4 %fusion.14 = f32[256,128]{1,0:T(8,128)S(1)} fusion(f32[256,128]{0,1:T(8,128)S(1)} %fusion.12, f32[128,256]{1,0:T(8,128)S(1)} %get-tuple-element.95, f32[128,256]{1,0:T(8,128)S(1)} %collective-permute-done, pred[]{:T(512)S(6)} %eq.24), kind=kOutput, calls=%fused_computation.24 | convolution fusion | flops 100859904 | bytes 524289 | tf_op jit(solution)/shard_map/dot_general | solution.py:75
  14.1 0.1 conditional.5
  14.3 0.4 %fusion.20 = f32[256,128]{1,0:T(8,128)S(1)} fusion(f32[256,128]{1,0:T(8,128)S(1)} %get-tuple-element.97, f32[128,256]{1,0:T(8,128)S(1)} %get-tuple-element.94, f32[128,256]{1,0:T(8,128)S(1)} %collective-permute-done.1, pred[]{:T(512)S(6)} %eq.23), kind=kOutput, calls=%fused_computation.31 | convolution fusion | flops 100859904 | bytes 524289 | tf_op jit(solution)/shard_map/dot_general | solution.py:75
  14.7 0.4 %fusion.26 = f32[256,128]{1,0:T(8,128)S(1)} fusion(f32[256,128]{1,0:T(8,128)S(1)} %get-tuple-element.98, f32[128,256]{1,0:T(8,128)S(1)} %get-tuple-element.93, f32[128,256]{1,0:T(8,128)S(1)} %collective-permute-done.2, pred[]{:T(512)S(6)} %eq.22), kind=kOutput, calls=%fused_computation.38 | convolution fusion | flops 100859904 | bytes 524289 | tf_op jit(solution)/shard_map/dot_general | solution.py:80
  15.1 0.4 %fusion.32 = f32[256,128]{1,0:T(8,128)S(1)} fusion(f32[256,128]{1,0:T(8,128)S(1)} %get-tuple-element.99, f32[128,256]{1,0:T(8,128)S(1)} %get-tuple-element.96, f32[128,256]{1,0:T(8,128)S(1)} %collective-permute-done.3, pred[]{:T(512)S(6)} %eq.21), kind=kOutput, calls=%fused_computation.45 | convolution fusion | flops 100859904 | bytes 524289 | tf_op jit(solution)/shard_map/dot_general | solution.py:80
  15.6 0.4 %fusion.38 = f32[256,128]{1,0:T(8,128)S(1)} fusion(f32[256,128]{1,0:T(8,128)S(1)} %get-tuple-element.100, f32[128,256]{1,0:T(8,128)S(1)} %get-tuple-element.92, f32[128,256]{1,0:T(8,128)S(1)} %collective-permute-done.4, pred[]{:T(512)S(6)} %eq.25), kind=kOutput, calls=%fused_computation.52 | convolution fusion | flops 100859904 | bytes 524289 | tf_op jit(solution)/shard_map/dot_general | solution.py:80
  16.1 0.8 %copy-done.2 = bf16[512,256]{1,0:T(8,128)(2,1)S(1)} copy-done((bf16[512,256]{1,0:T(8,128)(2,1)S(1)}, bf16[512,256]{1,0:T(8,128)(2,1)}, u32[]{:S(2)}) %copy-start.2) | copy-done | bytes 262168
  17.0 0.2 %fusion.45 = f32[128,256]{1,0:T(8,128)S(1)} fusion(bf16[512,256]{1,0:T(8,128)(2,1)S(1)} %copy-done.2, f32[256,128]{1,0:T(8,128)S(1)} %get-tuple-element.101), kind=kOutput, calls=%fused_computation.59 | convolution fusion | flops 16809984 | bytes 393216 | tf_op jit(solution)/shard_map/dot_general | solution.py:88
  17.2 0.4 %convolution_convert_fusion = bf16[128,256]{1,0:T(8,128)(2,1)S(1)} fusion(f32[128,256]{1,0:T(8,128)S(1)} %fusion.45, f32[1,1,256,256]{3,2,1,0:T(8,128)S(1)} %copy-done), kind=kOutput, calls=%fused_computation.22 | convolution fusion | flops 100696064 | bytes 458752 | tf_op jit(solution)/shard_map/dot_general | solution.py:91
  17.6 0.2 %fusion.11 = bf16[512,128]{0,1:T(8,128)(2,1)S(1)} fusion(bf16[128,256]{1,0:T(8,128)(2,1)S(1)} %convolution_convert_fusion, bf16[512,256]{1,0:T(8,128)(2,1)S(1)} %copy-done.2, f32[256,128]{0,1:T(8,128)S(1)} %copy.11), kind=kOutput, calls=%fused_computation.17 | convolution fusion | flops 33685504 | bytes 589824 | tf_op jit(solution)/shard_map/dot_general | solution.py:92
  17.8 0.8 %copy.12 = bf16[512,128]{1,0:T(8,128)(2,1)} copy(bf16[512,128]{0,1:T(8,128)(2,1)S(1)} %fusion.11) | data formatting | bytes 262144 | tf_op jit(solution)/shard_map/convert_element_type | solution.py:94
  (27 shorter events, 0.6 us)
Async XLA Ops:
  0.0 17.2 %copy-start = (f32[1,1,256,256]{3,2,1,0:T(8,128)S(1)}, f32[1,1,256,256]{3,2,1,0:T(8,128)}, u32[]{:S(2)}) copy-start(f32[1,1,256,256]{3,2,1,0:T(8,128)} %param.24) | copy-start | bytes 786436
  0.0 10.0 %copy-start.3 = (f32[256,128]{1,0:T(8,128)S(1)}, f32[256,128]{1,0:T(8,128)}, u32[]{:S(2)}) copy-start(f32[256,128]{1,0:T(8,128)} %param.18) | copy-start | bytes 393220
  1.3 12.4 %collective-permute-start = (f32[128,256]{1,0:T(8,128)S(1)}, f32[128,256]{1,0:T(8,128)S(1)}, u32[]{:S(2)}, u32[]{:S(2)}) collective-permute-start(f32[128,256]{1,0:T(8,128)S(1)} %get-tuple-element.95), channel_id=1, source_target_pairs={{0,16},{16,0},{8,24},{24,8},{1,17},{17,1},{9,25},{25,9},{2,18},{18... | collective-permute-start | bytes 393224 | tf_op jit(solution)/shard_map/ppermute | solution.py:16
  4.3 10.0 %collective-permute-start.1 = (f32[128,256]{1,0:T(8,128)S(1)}, f32[128,256]{1,0:T(8,128)S(1)}, u32[]{:S(2)}, u32[]{:S(2)}) collective-permute-start(f32[128,256]{1,0:T(8,128)S(1)} %get-tuple-element.94), channel_id=1, source_target_pairs={{0,8},{8,0},{16,24},{24,16},{1,9},{9,1},{17,25},{25,17},{2,10},{10... | collective-permute-start | bytes 393224 | tf_op jit(solution)/shard_map/ppermute | solution.py:16
  4.3 10.4 %collective-permute-start.2 = (f32[128,256]{1,0:T(8,128)S(1)}, f32[128,256]{1,0:T(8,128)S(1)}, u32[]{:S(2)}, u32[]{:S(2)}) collective-permute-start(f32[128,256]{1,0:T(8,128)S(1)} %get-tuple-element.93), channel_id=1, source_target_pairs={{0,4},{4,0},{1,5},{5,1},{2,6},{6,2},{3,7},{7,3},{8,12},{12,8},{9,1... | collective-permute-start | bytes 393224 | tf_op jit(solution)/shard_map/ppermute | solution.py:16
  6.9 8.2 %collective-permute-start.3 = (f32[128,256]{1,0:T(8,128)S(1)}, f32[128,256]{1,0:T(8,128)S(1)}, u32[]{:S(2)}, u32[]{:S(2)}) collective-permute-start(f32[128,256]{1,0:T(8,128)S(1)} %get-tuple-element.96), channel_id=1, source_target_pairs={{0,2},{2,0},{1,3},{3,1},{4,6},{6,4},{5,7},{7,5},{8,10},{10,8},{9,1... | collective-permute-start | bytes 393224 | tf_op jit(solution)/shard_map/ppermute | solution.py:16
  8.5 7.1 %collective-permute-start.4 = (f32[128,256]{1,0:T(8,128)S(1)}, f32[128,256]{1,0:T(8,128)S(1)}, u32[]{:S(2)}, u32[]{:S(2)}) collective-permute-start(f32[128,256]{1,0:T(8,128)S(1)} %get-tuple-element.92), channel_id=1, source_target_pairs={{0,1},{1,0},{2,3},{3,2},{4,5},{5,4},{6,7},{7,6},{8,9},{9,8},{10,11... | collective-permute-start | bytes 393224 | tf_op jit(solution)/shard_map/ppermute | solution.py:16
  10.0 0.9 %copy-start.4 = (bf16[2,256,128]{2,1,0:T(8,128)(2,1)S(1)}, bf16[2,256,128]{2,1,0:T(8,128)(2,1)}, u32[]{:S(2)}) copy-start(bf16[2,256,128]{2,1,0:T(8,128)(2,1)} %param.19) | copy-start | bytes 393220
  10.9 0.9 %copy-start.5 = (f32[2,128,128]{2,1,0:T(8,128)S(1)}, f32[2,128,128]{2,1,0:T(8,128)}, u32[]{:S(2)}) copy-start(f32[2,128,128]{2,1,0:T(8,128)} %param.20) | copy-start | bytes 393220
  12.3 1.8 %copy-start.1 = (bf16[1,1,5,256,256]{4,3,2,1,0:T(8,128)(2,1)S(1)}, bf16[1,1,5,256,256]{4,3,2,1,0:T(8,128)(2,1)}, u32[]{:S(2)}) copy-start(bf16[1,1,5,256,256]{4,3,2,1,0:T(8,128)(2,1)} %param.21) | copy-start | bytes 1966084
  16.0 1.0 %copy-start.2 = (bf16[512,256]{1,0:T(8,128)(2,1)S(1)}, bf16[512,256]{1,0:T(8,128)(2,1)}, u32[]{:S(2)}) copy-start(bf16[512,256]{1,0:T(8,128)(2,1)} %param.23) | copy-start | bytes 786436
where the time goes:
time: 18.9 us; the launch traced here: 18.6 us
  starting transfers between devices  8.69 us (46%)
  local copies, waits for them, and re-layouts  4.59 us (24%)
  matrix products  4.17 us (22%)
  between operations  0.9 us (5%)
    ppermute x5, starting transfers between devices, from_partner(): return lax.ppermute(block, axis, route)  8.69 us
    unnamed x13, local copies, waits for them, and re-layouts  2.39 us
    dot_general x5, matrix products, on_device(): weighted = jnp.dot(full_factor, current, precision=highest)  1.88 us
    squeeze x1, local copies, waits for them, and re-layouts, on_device(): own_factors[height_index]  1.25 us
    convert_element_type x1, local copies, waits for them, and re-layouts, on_device(): return (extended - applied).astype(jnp.bfloat16)  0.76 us
    dot_general x2, matrix products, back_panels(): scaled = jnp.dot(panel_factors[panel_index], projected, precision=highest)  0.55 us
    dot_general x2, matrix products, back_panels(): result = result - jnp.dot(reflect, scaled, precision=highest)  0.46 us
    dot_general x2, matrix products, back_panels(): lax.dot_general(reflect, result, (((0,), (0,)), ((), ())), precision=high...  0.46 us
  transfers between devices with their start and end apart: 5, of which 0 were waited for; matrix products, arithmetic and copies ran while one was open for 17% of the time, Pallas kernels for 0%

commit v1 on v0

v1 whole, which is shorter than its diff:
```python
import jax
import jax.numpy as jnp
from jax import lax
from jax.experimental import pallas as pl
from jax.experimental.pallas import tpu as pltpu
from jax.sharding import PartitionSpec as P

MESH = pl.DeviceIdType.MESH
F32, BF16 = jnp.float32, jnp.bfloat16


def halves(x):
    high = x.astype(BF16)
    return high, (x - high.astype(F32)).astype(BF16)


def dot(a, b, contract=((1,), (0,))):
    return lax.dot_general(a, b, (contract, ((), ())), preferred_element_type=F32)


def dot_exact_left(a, b, contract=((1,), (0,))):
    n = b.shape[1]
    both = dot(a, jnp.concatenate(halves(b), axis=1), contract)
    return both[:, :n] + both[:, n:]


def dot_split(a_halves, b):
    a_high, a_low = a_halves
    b_high, b_low = halves(b)
    n = b.shape[1]
    both = dot(a_high, jnp.concatenate([b_high, b_low], axis=1))
    return both[:, :n] + both[:, n:] + dot(a_low, b_high)


def kernel(group_count, slot_count, left_ref, panel_v_ref, panel_f_ref, node_y_ref, node_t_ref,
           leaf_v_ref, leaf_t_ref, map_ref, out_ref,
           left, panel_v, panel_f, node_y, factor, leaf_v, leaf_t,
           in_sem, own_sem, send_sem, recv_sem):
    group_levels = group_count.bit_length() - 1
    leaf_levels = slot_count.bit_length() - 1
    levels = group_levels + leaf_levels
    half = node_t_ref.shape[3]
    n = node_t_ref.shape[4]
    g = lax.axis_index("group")
    j = lax.axis_index("leaf")

    sides, partners = [], []
    for level in range(levels):
        if level < group_levels:
            bit = 1 << (group_levels - 1 - level)
            side = lax.rem(g // bit, 2)
            partners.append((g + bit * (1 - 2 * side), j))
        else:
            bit = 1 << (levels - 1 - level)
            side = lax.rem(j // bit, 2)
            partners.append((g, j + bit * (1 - 2 * side)))
        sides.append(side)

    barrier = pltpu.get_barrier_semaphore()
    for partner in partners:
        pl.semaphore_signal(barrier, inc=1, device_id=partner, device_id_type=MESH)

    loads = [
        pltpu.make_async_copy(source, target, in_sem.at[k])
        for k, (source, target) in enumerate([
            (left_ref, left), (panel_v_ref, panel_v), (panel_f_ref, panel_f),
            (node_y_ref.at[0, 0], node_y), (leaf_v_ref, leaf_v), (leaf_t_ref.at[0, 0], leaf_t),
        ])
    ]
    for load in loads[:3]:
        load.start()
    rows = [pl.ds(pl.multiple_of(sides[level] * half, half), half) for level in range(levels)]
    own = [
        pltpu.make_async_copy(node_t_ref.at[0, 0, level], factor.at[level, rows[level]], own_sem.at[level])
        for level in range(levels)
    ]
    sends = [
        pltpu.make_async_remote_copy(
            src_ref=node_t_ref.at[0, 0, level], dst_ref=factor.at[level, rows[level]],
            send_sem=send_sem.at[level], recv_sem=recv_sem.at[level],
            device_id=partners[level], device_id_type=MESH)
        for level in range(levels)
    ]
    pl.semaphore_wait(barrier, levels)
    first = group_levels
    order = [first, 0] + list(range(levels - 1, first, -1)) + list(range(1, group_levels))
    for level in order:
        sends[level].start()
    for load in loads[3:]:
        load.start()
    for level in range(levels):
        own[level].start()

    for load in loads[:3]:
        load.wait()
    current = left[...]
    for p in range(panel_v_ref.shape[0] - 1, -1, -1):
        reflect = panel_v[p]
        projected = dot_exact_left(reflect, current, ((0,), (0,)))
        scaled = dot_split(halves(panel_f[p]), projected)
        current = current - dot_exact_left(reflect, scaled)

    for load in loads[3:]:
        load.wait()
    for level in range(levels):
        own[level].wait()

    diagonal = (lax.broadcasted_iota(jnp.int32, (n, n), 0)
                == lax.broadcasted_iota(jnp.int32, (n, n), 1))
    identity = jnp.where(diagonal, 1.0, 0.0)
    flipped = jnp.minimum(jnp.abs(map_ref[0, 0] - j), 1)
    odd = lax.rem(j, 2)
    last = odd + flipped - 2 * odd * flipped

    lower = [side.astype(F32) for side in sides[:-1]] + [last.astype(F32)]

    def spread(level):
        f = lower[level]
        return (node_y[level].astype(F32) * f + identity * (1.0 - f)).astype(BF16)

    def step(level, x):
        weighted = dot_split(halves(factor[level]), x)
        return x * (1.0 - lower[level]) - dot_exact_left(spread(level), weighted)

    for level in range(levels):
        sends[level].wait()
        current = step(level, current)

    rounded = current.astype(BF16)
    projected = dot(leaf_v[:n], rounded, ((0,), (0,)))
    solved = dot_split(halves(leaf_t[...]), projected).astype(BF16)
    out_ref[:n] = (current - dot(leaf_v[:n], solved)).astype(BF16)
    out_ref[n:] = (-dot(leaf_v[n:], solved)).astype(BF16)


def solution(mesh):
    group_count, slot_count = mesh.shape["group"], mesh.shape["leaf"]

    def on_device(left, panel_v, panel_f, node_y, node_t, leaf_v, leaf_t, leaf_map):
        levels, n = node_y.shape[2], node_y.shape[3]
        anywhere = pl.BlockSpec(memory_space=pltpu.HBM)

        def body(*refs):
            kernel(group_count, slot_count, *refs)

        return pl.pallas_call(
            body,
            out_shape=jax.ShapeDtypeStruct((leaf_v.shape[0], left.shape[1]), BF16),
            in_specs=[anywhere] * 7 + [pl.BlockSpec(memory_space=pltpu.SMEM)],
            out_specs=pl.BlockSpec(memory_space=pltpu.VMEM),
            scratch_shapes=[
                pltpu.VMEM(left.shape, F32),
                pltpu.VMEM(panel_v.shape, BF16),
                pltpu.VMEM(panel_f.shape, F32),
                pltpu.VMEM((levels, n, n), BF16),
                pltpu.VMEM((levels, n, n), F32),
                pltpu.VMEM(leaf_v.shape, BF16),
                pltpu.VMEM((n, n), F32),
                pltpu.SemaphoreType.DMA((6,)),
                pltpu.SemaphoreType.DMA((levels,)),
                pltpu.SemaphoreType.DMA((levels,)),
                pltpu.SemaphoreType.DMA((levels,)),
            ],
            compiler_params=pltpu.CompilerParams(
                collective_id=0, has_side_effects=True, vmem_limit_bytes=64512 * 1024),
        )(left, panel_v, panel_f, node_y, node_t, leaf_v, leaf_t, leaf_map)

    return jax.shard_map(
        on_device,
        mesh=mesh,
        in_specs=(
            P(), P(), P(),
            P("group", "leaf", None, None, None),
            P("group", "leaf", None, None, None),
            P(("group", "leaf"), None),
            P("group", "leaf", None, None),
            P("group", "leaf"),
        ),
        out_specs=P(("group", "leaf"), None),
        check_vma=False,
    )
```

time: 18.9 us -> 17 us (0.90)
  Pallas kernels: 0 us -> 14.6 us
  starting transfers between devices: 8.69 us -> 0 us
  matrix products: 4.17 us -> 0 us
  local copies, waits for them, and re-layouts: 4.59 us -> 1.57 us
  between operations: 0.9 us -> 0.66 us
    pallas_call x0 -> x1, Pallas kernels: none -> 14.6 us  [on_device(): pl.pallas_call(body, out_shape=jax.ShapeDtypeStruct((leaf_v.shape[0], lef...]
    ppermute x5 -> x0, starting transfers between devices: 8.69 us -> none  [from_partner(): return lax.ppermute(block, axis, route)]
    dot_general x14 -> x0, matrix products: 4.17 us -> none  [the longest x5 1.88 us: on_device(): weighted = jnp.dot(full_factor, current, precision=highest)]
    squeeze x1 -> x0, local copies, waits for them, and re-layouts: 1.25 us -> none  [on_device(): own_factors[height_index]]
    unnamed x13 -> x1, local copies, waits for them, and re-layouts: 2.39 us -> 1.57 us
    convert_element_type x1 -> x0, local copies, waits for them, and re-layouts: 0.76 us -> none  [on_device(): return (extended - applied).astype(jnp.bfloat16)]
  transfers between devices with their start and end apart: 5 -> 0, of which waited for: 0 -> 0; matrix products, arithmetic and copies ran while one was open for 17% -> 0% of each run, Pallas kernels for 0% -> 0%
where the time goes in v1:
time: 17 us; the launch traced here: 16.8 us
  Pallas kernels  14.6 us (86%)
  local copies, waits for them, and re-layouts  1.57 us (9%)
  between operations  0.66 us (4%)
    pallas_call x1, Pallas kernels, on_device(): pl.pallas_call(body, out_shape=jax.ShapeDtypeStruct((leaf_v.shape[0], lef...  14.6 us
    unnamed x1, local copies, waits for them, and re-layouts  1.57 us

profile of v1, /device:TPU:0, one launch (start us, length us, event | category | flops | bytes accessed | tf_op | source)
XLA Modules:
  0.0 16.8 jit_solution(9424093388026636253)
XLA Ops:
  0.7 14.6 %shard_map.82 = bf16[512,128]{1,0:T(8,128)(2,1)} custom-call(f32[256,128]{1,0:T(8,128)} %refs_0_.1, bf16[2,256,128]{2,1,0:T(8,128)(2,1)} %refs_1_.1, f32[2,128,128]{2,1,0:T(8,128)} %refs_2_.1, bf16[1,1,5,256,256]{4,3,2,1,0:T(8,128)(2,1)} %refs_3_.1, f32[1,1,5,128,256]{4,3,2,1,0:T(8,128)} %refs_4_.1, bf16[512,256]{1,0:T(8,128)(2,1)} %refs_5_.1, ...), custom_call_target="tpu_custom_call" | custom-call | tf_op jit(solution)/shard_map/pallas_call | solution.py:146
  15.3 1.6 %copy.11 = bf16[512,128]{1,0:T(8,128)(2,1)} copy(bf16[512,128]{1,0:T(8,128)(2,1)} %shard_map.82) | data formatting | bytes 262144

commit v2 on v1

--- a/solution.py
+++ b/solution.py
@@ -74,17 +74,30 @@
         pltpu.make_async_copy(node_t_ref.at[0, 0, level], factor.at[level, rows[level]], own_sem.at[level])
         for level in range(levels)
     ]
+    first = group_levels
+    quarter = half // 2
+    mine = lax.rem(j, 2) * quarter
+
+    def send(source, target, partner, slot):
+        return pltpu.make_async_remote_copy(
+            src_ref=source, dst_ref=target, send_sem=send_sem.at[slot], recv_sem=recv_sem.at[slot],
+            device_id=partner, device_id_type=MESH)
+
     sends = [
-        pltpu.make_async_remote_copy(
-            src_ref=node_t_ref.at[0, 0, level], dst_ref=factor.at[level, rows[level]],
-            send_sem=send_sem.at[level], recv_sem=recv_sem.at[level],
-            device_id=partners[level], device_id_type=MESH)
+        send(node_t_ref.at[0, 0, level], factor.at[level, rows[level]], partners[level], level)
         for level in range(levels)
     ]
+    cross_rows = pl.ds(pl.multiple_of(sides[first] * half + mine, quarter), quarter)
+    sends[first] = send(
+        node_t_ref.at[0, 0, first, pl.ds(pl.multiple_of(mine, quarter), quarter)],
+        factor.at[first, cross_rows], partners[first], first)
+    pass_rows = factor.at[first, pl.ds(pl.multiple_of((1 - sides[first]) * half + mine, quarter), quarter)]
+    passed = send(pass_rows, pass_rows, partners[levels - 1], levels)
     pl.semaphore_wait(barrier, levels)
-    first = group_levels
-    order = [first, 0] + list(range(levels - 1, first, -1)) + list(range(1, group_levels))
-    for level in order:
+    early = [first, 0, levels - 1] + list(range(1, group_levels))
+    for level in early:
+        sends[level].start()
+    for level in range(first + 1, levels - 1):
         sends[level].start()
     for load in loads[3:]:
         load.start()
@@ -122,13 +135,30 @@
         weighted = dot_split(halves(factor[level]), x)
         return x * (1.0 - lower[level]) - dot_exact_left(spread(level), weighted)
 
-    for level in range(levels):
+    def whole_step(level):
+        return identity * (1.0 - lower[level]) - dot_exact_left(spread(level), factor[level])
+
+    top = leaf_v[:n]
+    solver_high, solver_low = halves(leaf_t[...])
+    solver = dot(solver_high, top, ((1,), (1,))) + dot(solver_low, top, ((1,), (1,)))
+    solver_high, solver_low = halves(solver)
+
+    sends[first].wait_recv()
+    passed.start()
+    for level in range(first):
         sends[level].wait()
         current = step(level, current)
+    rest = None
+    for level in range(levels - 1, first, -1):
+        sends[level].wait()
+        one = whole_step(level)
+        rest = halves(one if rest is None else dot_split(rest, one))
+    sends[first].wait_send()
+    passed.wait()
+    current = dot_split(rest, step(first, current))
 
     rounded = current.astype(BF16)
-    projected = dot(leaf_v[:n], rounded, ((0,), (0,)))
-    solved = dot_split(halves(leaf_t[...]), projected).astype(BF16)
+    solved = (dot(solver_high, rounded) + dot(solver_low, rounded)).astype(BF16)
     out_ref[:n] = (current - dot(leaf_v[:n], solved)).astype(BF16)
     out_ref[n:] = (-dot(leaf_v[n:], solved)).astype(BF16)
 
@@ -139,6 +169,8 @@
     def on_device(left, panel_v, panel_f, node_y, node_t, leaf_v, leaf_t, leaf_map):
         levels, n = node_y.shape[2], node_y.shape[3]
         anywhere = pl.BlockSpec(memory_space=pltpu.HBM)
+
+        pin = lambda x: pltpu.with_memory_space_constraint(x, pltpu.HBM)
 
         def body(*refs):
             kernel(group_count, slot_count, *refs)
@@ -158,12 +190,12 @@
                 pltpu.VMEM((n, n), F32),
                 pltpu.SemaphoreType.DMA((6,)),
                 pltpu.SemaphoreType.DMA((levels,)),
-                pltpu.SemaphoreType.DMA((levels,)),
-                pltpu.SemaphoreType.DMA((levels,)),
+                pltpu.SemaphoreType.DMA((levels + 1,)),
+                pltpu.SemaphoreType.DMA((levels + 1,)),
             ],
             compiler_params=pltpu.CompilerParams(
-                collective_id=0, has_side_effects=True, vmem_limit_bytes=64512 * 1024),
-        )(left, panel_v, panel_f, node_y, node_t, leaf_v, leaf_t, leaf_map)
+                collective_id=0, has_side_effects=True, vmem_limit_bytes=40 * 1024 * 1024),
+        )(*map(pin, (left, panel_v, panel_f, node_y, node_t, leaf_v, leaf_t)), leaf_map)
 
     return jax.shard_map(
         on_device,

time: 17 us -> 15.4 us (0.906)
  local copies, waits for them, and re-layouts: 1.57 us -> 0.66 us
  Pallas kernels: 14.6 us -> 13.9 us
    unnamed x1, local copies, waits for them, and re-layouts: 1.57 us -> 0.66 us
    pallas_call x1, Pallas kernels: 14.6 us -> 13.9 us  [on_device(): pl.pallas_call(body, out_shape=jax.ShapeDtypeStruct((leaf_v.shape[0], lef...]
where the time goes in v2:
time: 15.4 us; the launch traced here: 15.2 us
  Pallas kernels  13.9 us (90%)
  local copies, waits for them, and re-layouts  0.66 us (4%)
  between operations  0.66 us (4%)
    pallas_call x1, Pallas kernels, on_device(): pl.pallas_call(body, out_shape=jax.ShapeDtypeStruct((leaf_v.shape[0], lef...  13.9 us
    unnamed x1, local copies, waits for them, and re-layouts  0.66 us

profile of v2, /device:TPU:0, one launch (start us, length us, event | category | flops | bytes accessed | tf_op | source)
XLA Modules:
  0.0 15.2 jit_solution(7656781022604439633)
XLA Ops:
  0.7 13.9 %shard_map.82 = bf16[512,128]{1,0:T(8,128)(2,1)S(1)} custom-call(f32[256,128]{1,0:T(8,128)} %refs_0_.1, bf16[2,256,128]{2,1,0:T(8,128)(2,1)} %refs_1_.1, f32[2,128,128]{2,1,0:T(8,128)} %refs_2_.1, bf16[1,1,5,256,256]{4,3,2,1,0:T(8,128)(2,1)} %refs_3_.1, f32[1,1,5,128,256]{4,3,2,1,0:T(8,128)} %refs_4_.1, bf16[512,256]{1,0:T(8,128)(2,1)} %refs_5_.1, ...), custom_call_target="tpu_custom_call" | custom-call | tf_op jit(solution)/shard_map/pallas_call | solution.py:178
  14.6 0.7 %copy.11 = bf16[512,128]{1,0:T(8,128)(2,1)} copy(bf16[512,128]{1,0:T(8,128)(2,1)S(1)} %shard_map.82) | data formatting | bytes 262144

commit v3 on v2

--- a/solution.py
+++ b/solution.py
@@ -7,6 +7,7 @@
 
 MESH = pl.DeviceIdType.MESH
 F32, BF16 = jnp.float32, jnp.bfloat16
+PIECES = 4
 
 
 def halves(x):
@@ -67,42 +68,54 @@
             (node_y_ref.at[0, 0], node_y), (leaf_v_ref, leaf_v), (leaf_t_ref.at[0, 0], leaf_t),
         ])
     ]
-    for load in loads[:3]:
-        load.start()
     rows = [pl.ds(pl.multiple_of(sides[level] * half, half), half) for level in range(levels)]
     own = [
         pltpu.make_async_copy(node_t_ref.at[0, 0, level], factor.at[level, rows[level]], own_sem.at[level])
         for level in range(levels)
     ]
+    for level in [group_levels, 0, levels - 1] + list(range(1, group_levels)) + list(range(group_levels + 1, levels - 1)):
+        own[level].start()
+    for load in loads[:3]:
+        load.start()
+
     first = group_levels
     quarter = half // 2
-    mine = lax.rem(j, 2) * quarter
 
     def send(source, target, partner, slot):
         return pltpu.make_async_remote_copy(
             src_ref=source, dst_ref=target, send_sem=send_sem.at[slot], recv_sem=recv_sem.at[slot],
             device_id=partner, device_id_type=MESH)
 
+    def relay(level, pair_level, pieces, slot):
+        piece = quarter // pieces
+        crossed, passed = [], []
+        for k in range(pieces):
+            begin = sides[pair_level] * quarter + k * piece
+            leaving = factor.at[level, pl.ds(pl.multiple_of(sides[level] * half + begin, piece), piece)]
+            arrived = factor.at[level, pl.ds(pl.multiple_of((1 - sides[level]) * half + begin, piece), piece)]
+            crossed.append(send(leaving, leaving, partners[level], slot + k))
+            passed.append(send(arrived, arrived, partners[pair_level], slot + pieces + k))
+        return crossed, passed
+
     sends = [
-        send(node_t_ref.at[0, 0, level], factor.at[level, rows[level]], partners[level], level)
+        send(factor.at[level, rows[level]], factor.at[level, rows[level]], partners[level], level)
+        if level != first else None
         for level in range(levels)
     ]
-    cross_rows = pl.ds(pl.multiple_of(sides[first] * half + mine, quarter), quarter)
-    sends[first] = send(
-        node_t_ref.at[0, 0, first, pl.ds(pl.multiple_of(mine, quarter), quarter)],
-        factor.at[first, cross_rows], partners[first], first)
-    pass_rows = factor.at[first, pl.ds(pl.multiple_of((1 - sides[first]) * half + mine, quarter), quarter)]
-    passed = send(pass_rows, pass_rows, partners[levels - 1], levels)
+    crossed, passed = relay(first, levels - 1, PIECES, levels)
     pl.semaphore_wait(barrier, levels)
-    early = [first, 0, levels - 1] + list(range(1, group_levels))
+    own[first].wait()
+    for copy in crossed:
+        copy.start()
+    early = [0, levels - 1] + list(range(1, group_levels))
     for level in early:
+        own[level].wait()
         sends[level].start()
     for level in range(first + 1, levels - 1):
+        own[level].wait()
         sends[level].start()
     for load in loads[3:]:
         load.start()
-    for level in range(levels):
-        own[level].start()
 
     for load in loads[:3]:
         load.wait()
@@ -115,8 +128,6 @@
 
     for load in loads[3:]:
         load.wait()
-    for level in range(levels):
-        own[level].wait()
 
     diagonal = (lax.broadcasted_iota(jnp.int32, (n, n), 0)
                 == lax.broadcasted_iota(jnp.int32, (n, n), 1))
@@ -143,8 +154,9 @@
     solver = dot(solver_high, top, ((1,), (1,))) + dot(solver_low, top, ((1,), (1,)))
     solver_high, solver_low = halves(solver)
 
-    sends[first].wait_recv()
-    passed.start()
+    for k in range(PIECES):
+        crossed[k].wait_recv()
+        passed[k].start()
     for level in range(first):
         sends[level].wait()
         current = step(level, current)
@@ -153,9 +165,13 @@
         sends[level].wait()
         one = whole_step(level)
         rest = halves(one if rest is None else dot_split(rest, one))
-    sends[first].wait_send()
-    passed.wait()
-    current = dot_split(rest, step(first, current))
+    kept = dot_split(rest, current) * (1.0 - lower[first])
+    onward = halves(dot(rest[0], spread(first)) + dot(rest[1], spread(first)))
+    for copy in crossed:
+        copy.wait_send()
+    for copy in passed:
+        copy.wait()
+    current = kept - dot_split(onward, dot_split(halves(factor[first]), current))
 
     rounded = current.astype(BF16)
     solved = (dot(solver_high, rounded) + dot(solver_low, rounded)).astype(BF16)
@@ -190,8 +206,8 @@
                 pltpu.VMEM((n, n), F32),
                 pltpu.SemaphoreType.DMA((6,)),
                 pltpu.SemaphoreType.DMA((levels,)),
-                pltpu.SemaphoreType.DMA((levels + 1,)),
-                pltpu.SemaphoreType.DMA((levels + 1,)),
+                pltpu.SemaphoreType.DMA((levels + 2 * PIECES,)),
+                pltpu.SemaphoreType.DMA((levels + 2 * PIECES,)),
             ],
             compiler_params=pltpu.CompilerParams(
                 collective_id=0, has_side_effects=True, vmem_limit_bytes=40 * 1024 * 1024),

time: 15.4 us -> 14.6 us (0.948)
  Pallas kernels: 13.9 us -> 13.1 us
    pallas_call x1, Pallas kernels: 13.9 us -> 13.1 us  [on_device(): pl.pallas_call(body, out_shape=jax.ShapeDtypeStruct((leaf_v.shape[0], lef...]
where the time goes in v3:
time: 14.6 us; the launch traced here: 14.4 us
  Pallas kernels  13.1 us (90%)
  local copies, waits for them, and re-layouts  0.66 us (5%)
  between operations  0.66 us (5%)
    pallas_call x1, Pallas kernels, on_device(): pl.pallas_call(body, out_shape=jax.ShapeDtypeStruct((leaf_v.shape[0], lef...  13.1 us
    unnamed x1, local copies, waits for them, and re-layouts  0.66 us

profile of v3, /device:TPU:0, one launch (start us, length us, event | category | flops | bytes accessed | tf_op | source)
XLA Modules:
  0.0 14.4 jit_solution(11017388208719551671)
XLA Ops:
  0.7 13.1 %shard_map.82 = bf16[512,128]{1,0:T(8,128)(2,1)S(1)} custom-call(f32[256,128]{1,0:T(8,128)} %refs_0_.1, bf16[2,256,128]{2,1,0:T(8,128)(2,1)} %refs_1_.1, f32[2,128,128]{2,1,0:T(8,128)} %refs_2_.1, bf16[1,1,5,256,256]{4,3,2,1,0:T(8,128)(2,1)} %refs_3_.1, f32[1,1,5,128,256]{4,3,2,1,0:T(8,128)} %refs_4_.1, bf16[512,256]{1,0:T(8,128)(2,1)} %refs_5_.1, ...), custom_call_target="tpu_custom_call" | custom-call | tf_op jit(solution)/shard_map/pallas_call | solution.py:194
  13.8 0.7 %copy.11 = bf16[512,128]{1,0:T(8,128)(2,1)} copy(bf16[512,128]{1,0:T(8,128)(2,1)S(1)} %shard_map.82) | data formatting | bytes 262144
